TPU v7x, 256 devices: a whole 4x4x8 slice. The times are simulated.
256 devices in a mesh: tm: 16 (over x, y), pts: 16 (over z, core).
Axes of the slice: x: 4, y: 4, z: 8, core: 2. Of those that a mesh axis runs over, the one named last changes fastest.
Arguments:
- feats: bfloat16 [16, 4096, 256], P('tm', 'pts'), may hold values from -24 to 24
- query_frame: int32 [16384], P('pts'), may hold values from 0 to 15
- query_pos: int32 [16384], P('pts'), may hold values from 0 to 4095
- time_mix: float32 [16, 16], replicated, may hold values from -1.5 to 1.5
- w_up: bfloat16 [512, 2048], replicated, may hold values from -0.25 to 0.25
- w_down: bfloat16 [2048, 512], replicated, may hold values from -0.125 to 0.125
- w_query: bfloat16 [512, 256], replicated, may hold values from -0.25 to 0.25
Outputs:
- track_x: float32 [16, 16384], P('tm', 'pts')
- track_y: float32 [16, 16384], P('tm', 'pts')
All inputs are finite; a program needn't handle non-finite values.
Results may differ from a plain program's by a relative error of at most 0.04.
Values may be sent and summed in bfloat16 or wider, within the bound.
No kernel may reach another device: no remote copies, remote signals or barrier semaphores. Data moves between devices by JAX's collectives and lax.ppermute only.
A program may use at most 64 MiB of HBM per device.

v0:
```python
import jax
import jax.numpy as jnp
from jax import lax
from jax.sharding import PartitionSpec as P

GRID = 64
HW = 4096


def rms_rows(values):
    return values * lax.rsqrt(jnp.mean(values * values, axis=-1, keepdims=True) + 1e-06)


def mixer(tokens, time_mix, w_up, w_down, w_query):
    frames, count, width = tokens.shape
    floats = tokens.astype(jnp.float32)
    normed = rms_rows(floats).astype(jnp.bfloat16)
    blended = jnp.einsum(
        "fg,gkd->fkd", time_mix, normed.astype(jnp.float32), precision=lax.Precision.HIGHEST
    )
    section = (floats + blended).astype(jnp.bfloat16)
    flat = section.reshape(frames * count, width)
    inner = rms_rows(flat.astype(jnp.float32)).astype(jnp.bfloat16)
    upper = jax.nn.gelu(jnp.dot(inner, w_up, preferred_element_type=jnp.float32)).astype(
        jnp.bfloat16
    )
    mixed = (
        flat.astype(jnp.float32) + jnp.dot(upper, w_down, preferred_element_type=jnp.float32)
    ).astype(jnp.bfloat16)
    delta = jnp.dot(mixed, w_query, preferred_element_type=jnp.float32).astype(jnp.bfloat16)
    return delta.reshape(frames, count, w_query.shape[1])


def grid_coords():
    index = jnp.arange(HW, dtype=jnp.int32)
    xs = (2 * (index % GRID) + 1).astype(jnp.float32) / GRID - 1.0
    ys = (2 * (index // GRID) + 1).astype(jnp.float32) / GRID - 1.0
    return (xs, ys)


def row_scores(rows, piece, scale):
    return jnp.einsum("pc,jc->pj", rows, piece, preferred_element_type=jnp.float32) * scale


def soft_parts(scores):
    top = jnp.max(scores, axis=1, keepdims=True)
    expo = jnp.exp(scores - top)
    return (expo, jnp.sum(expo, axis=1, keepdims=True))


def shards(feats, query_frame, query_pos, time_mix, w_up, w_down, w_query):
    tile = feats[0]
    points = query_frame.shape[0]
    width = tile.shape[1]
    scale = width ** (-0.5)
    frame_id = lax.axis_index("tm")
    groups = lax.axis_size("tm")
    xs, ys = grid_coords()
    block = min(512, points)
    frame = lax.all_gather(tile, "pts", axis=0, tiled=True)
    picked = jnp.take(frame, query_pos, axis=0)
    own = jnp.where((query_frame == frame_id)[:, None], picked, jnp.zeros_like(picked))
    query = lax.psum(own, "tm").astype(jnp.float32).astype(jnp.bfloat16)
    pieces = []
    for first in range(0, points, block):
        expo, total = soft_parts(row_scores(query[first : first + block], frame, scale))
        product = jnp.dot(expo.astype(jnp.bfloat16), frame, preferred_element_type=jnp.float32)
        pieces.append((product / total).astype(jnp.bfloat16))
    matched = jnp.concatenate(pieces, axis=0)
    tokens = jnp.concatenate([matched, query], axis=1)
    tokens = tokens.reshape(1, groups, points // groups, tokens.shape[1])
    exchanged = lax.all_to_all(tokens, "tm", split_axis=1, concat_axis=0, tiled=True)
    frames_here = exchanged.shape[0]
    count = exchanged.shape[2]
    result = mixer(
        exchanged.reshape(frames_here, count, exchanged.shape[3]), time_mix, w_up, w_down, w_query
    )
    delta = result.reshape(frames_here, 1, count, result.shape[2])
    returned = lax.all_to_all(delta, "tm", split_axis=0, concat_axis=1, tiled=True)
    returned = returned.reshape(points, returned.shape[3])
    refined = (query.astype(jnp.float32) + returned.astype(jnp.float32)).astype(jnp.bfloat16)
    parts_x = []
    parts_y = []
    for first in range(0, points, block):
        expo, total = soft_parts(row_scores(refined[first : first + block], frame, scale))
        parts_x.append(jnp.sum(expo * xs, axis=1) / total[:, 0])
        parts_y.append(jnp.sum(expo * ys, axis=1) / total[:, 0])
    track_x = jnp.concatenate(parts_x, axis=0)
    track_y = jnp.concatenate(parts_y, axis=0)
    return (track_x[None], track_y[None])


def solution(mesh):
    placed = (P("tm", "pts", None), P("pts"), P("pts"), P(), P(), P(), P())
    return jax.shard_map(
        shards,
        mesh=mesh,
        in_specs=placed,
        out_specs=(P("tm", "pts"), P("tm", "pts")),
        check_vma=False,
    )
```

profile of v0, /device:TPU:8, one launch (start us, length us, event | category | flops | bytes accessed | tf_op | source)
XLA Modules:
  0.0 237.1 jit_solution(5785757866568762552)
XLA Ops:
  8.0 0.7 fusion.75
  8.7 0.7 compare_and_fusion
  9.4 43.1 %all-gather.3.cloned.1.call-done = bf16[1,4096,256]{2,1,0:T(8,128)(2,1)} async-done(((bf16[1,256,256]{2,1,0:T(8,128)(2,1)}), bf16[1,4096,256]{2,1,0:T(8,128)(2,1)}) %all-gather.3.cloned.1.call-update) | async-done | bytes 2097168 | tf_op jit(solution)/shard_map/all_gather | solution.py:60
  52.5 5.3 %gather_fusion = bf16[1024,256]{1,0:T(8,128)(2,1)S(1)} fusion(bf16[4096,256]{1,0:T(8,128)(2,1)} %bitcast.62, s32[1024]{0:T(1024)S(1)} %fusion.75), kind=kCustom, calls=%fused_computation | custom fusion | bytes 1052672 | tf_op jit(solution)/shard_map/jit(_take)/gather | solution.py:61
  57.8 1.2 select_select_fusion
  59.0 93.3 %all-reduce.2.cloned.1.call-done = bf16[1024,256]{1,0:T(8,128)(2,1)} async-done(((bf16[1024,256]{1,0:T(8,128)(2,1)}), bf16[1024,256]{1,0:T(8,128)(2,1)}) %all-reduce.2.cloned.1.call-update) | async-done | bytes 524304 | tf_op jit(solution)/shard_map/psum | solution.py:63
  152.3 3.2 %multiply_reduce_fusion.7 = (f32[512]{0:T(512)S(1)}, f32[512,4096]{1,0:T(8,128)S(1)}) fusion(bf16[1,4096,256]{2,1,0:T(8,128)(2,1)} %all-gather.3.cloned.1.call-done, bf16[1024,256]{1,0:T(8,128)(2,1)} %all-reduce.2.cloned.1.call-done), kind=kOutput, calls=%fused_computation.21 | convolution fusion | flops 1077935616 | bytes 10749952 | tf_op jit(solution)/shard_map/pc,jc->pj/dot_general | solution.py:42
  155.5 1.5 fusion.8
  157.0 1.4 multiply_reduce_fusion.6
  158.4 1.5 fusion.10
  159.9 1.5 fusion.37
  161.4 1.5 fusion.43
  163.0 19.4 %all_to_all.8 = bf16[1,16,64,512]{3,2,0,1:T(8,128)(2,1)S(1)} all-to-all(bf16[1,16,64,512]{3,2,0,1:T(8,128)(2,1)S(1)} %bitcast.63), channel_id=1, replica_groups=mesh['tm'=16,'pts'=16] {'tm'}, dimensions={1} | all-to-all | bytes 2097152 | tf_op jit(solution)/shard_map/all_to_all | solution.py:72
  182.4 1.0 copy-done.4
  184.2 4.3 %multiply_reduce_fusion.8 = (f32[16,64]{0,1:T(8,128)S(1)}, f32[16,64,512]{2,0,1:T(8,128)S(1)}) fusion(f32[16,16]{1,0:T(8,128)S(1)} %copy-done.6, f32[16,64]{0,1:T(8,128)S(1)} %copy.21, bf16[1,16,64,512]{3,2,0,1:T(8,128)(2,1)} %copy-done.4), kind=kOutput, calls=%fused_computation.45 | convolution fusion | flops 105380864 | bytes 3154944 | tf_op jit(solution)/shard_map/fg,gkd->fkd/dot_general | solution.py:18
  188.5 2.5 %copy.22 = f32[16,64,512]{2,1,0:T(8,128)} copy(f32[16,64,512]{2,0,1:T(8,128)S(1)} %get-tuple-element.20) | data formatting | bytes 4194304 | tf_op jit(solution)/shard_map/convert_element_type | solution.py:28
  191.1 2.8 %fusion.27 = bf16[1024,512]{1,0:T(8,128)(2,1)} fusion(f32[16,64,512]{2,1,0:T(8,128)} %copy.22, f32[1024]{0:T(1024)S(1)} %rsqrt.21), kind=kLoop, calls=%fused_computation.43 | loop fusion | flops 1048576 | bytes 3149824 | tf_op jit(solution)/shard_map/convert_element_type | solution.py:23
  194.0 8.3 %fusion.28 = bf16[1024,512]{1,0:T(8,128)(2,1)} fusion(f32[16,64,512]{2,1,0:T(8,128)} %copy.22, bf16[2048,512]{1,0:T(8,128)(2,1)S(1)} %copy-done, bf16[1024,512]{1,0:T(8,128)(2,1)} %fusion.27, bf16[512,2048]{1,0:T(8,128)(2,1)} %param.11), kind=kOutput, calls=%fused_computation.44 | convolution fusion | flops 4314890240 | bytes 8388608 | tf_op jit(solution)/shard_map/dot_general | solution.py:28
  202.3 2.5 %convolution_convert_fusion = bf16[1024,256]{1,0:T(8,128)(2,1)} fusion(bf16[1024,512]{1,0:T(8,128)(2,1)} %fusion.28, bf16[512,256]{1,0:T(8,128)(2,1)S(1)} %copy-done.5), kind=kOutput, calls=%fused_computation.48 | convolution fusion | flops 268697600 | bytes 1835008 | tf_op jit(solution)/shard_map/dot_general | solution.py:30
  204.7 4.8 %all-to-all-start.1 = ((bf16[16,1,64,256]{3,2,1,0:T(8,128)(2,1)}), bf16[16,1,64,256]{3,2,1,0:T(8,128)(2,1)S(1)}, u32[]{:S(2)}, u32[]{:S(2)}) async-start(bf16[16,1,64,256]{3,2,1,0:T(8,128)(2,1)} %bitcast.64), calls=%async_computation.1 | async-start | bytes 1048576 | tf_op jit(solution)/shard_map/all_to_all | solution.py:79
  209.6 8.8 %all-to-all-done.1 = bf16[16,1,64,256]{3,2,1,0:T(8,128)(2,1)S(1)} async-done(((bf16[16,1,64,256]{3,2,1,0:T(8,128)(2,1)}), bf16[16,1,64,256]{3,2,1,0:T(8,128)(2,1)S(1)}, u32[]{:S(2)}, u32[]{:S(2)}) %all-to-all-start.1) | async-done | bytes 524320 | tf_op jit(solution)/shard_map/all_to_all | solution.py:79
  218.6 3.1 %multiply_reduce_fusion.5 = (f32[512]{0:T(512)S(1)}, f32[512,4096]{1,0:T(8,128)S(1)}) fusion(bf16[1,4096,256]{2,1,0:T(8,128)(2,1)} %all-gather.3.cloned.1.call-done, bf16[1024,256]{1,0:T(8,128)(2,1)S(1)} %fusion.47), kind=kOutput, calls=%fused_computation.19 | convolution fusion | flops 1077935616 | bytes 10749952 | tf_op jit(solution)/shard_map/pc,jc->pj/dot_general | solution.py:42
  221.7 1.4 multiply_reduce_fusion.4
  223.0 6.0 %multiply_reduce_fusion = (f32[512]{0:T(512)S(1)}, f32[512]{0:T(512)S(1)}, f32[512]{0:T(512)S(1)}, f32[512]{0:T(512)S(1)}, f32[512]{0:T(512)S(1)}, /*index=5*/f32[512]{0:T(512)S(1)}) fusion(f32[512,4096]{1,0:T(8,128)S(1)} %get-tuple-element.22, f32[4096]{0:T(1024)S(1)} %get-tuple-element.28, f32[512]{0:T(512)S(1)} %get-tuple-element.21, ...), kind=kLoop, calls=%fused_computation.10 | loop fusion | flops 29357056 | bytes 16826368 | tf_op jit(solution)/shard_map/reduce_sum | solution.py:87
  (31 shorter events, 3.2 us)
Async XLA Ops:
  7.2 186.8 %copy-start = (bf16[2048,512]{1,0:T(8,128)(2,1)S(1)}, bf16[2048,512]{1,0:T(8,128)(2,1)}, u32[]{:S(2)}) copy-start(bf16[2048,512]{1,0:T(8,128)(2,1)} %param.12) | copy-start | bytes 6291460
  7.2 45.3 %all-gather.3.cloned.1.call-start = ((), (), s32[]{:S(2)}) async-start(), calls=%async_computation.3 | async-start | bytes 2228224 | tf_op jit(solution)/shard_map/all_gather | solution.py:60
  7.9 144.4 %all-reduce.2.cloned.1.call-start = ((), (), s32[]{:S(2)}) async-start(), calls=%async_computation.2 | async-start | bytes 1048576 | tf_op jit(solution)/shard_map/psum | solution.py:63
  152.3 4.7 %copy-start.1 = (bf16[1,4096,256]{2,1,0:T(8,128)(2,1)S(1)}, bf16[1,4096,256]{2,1,0:T(8,128)(2,1)}, u32[]{:S(2)}) copy-start(bf16[1,4096,256]{2,1,0:T(8,128)(2,1)} %all-gather.3.cloned.1.call-done) | copy-start | bytes 6291460
  152.3 4.7 %copy-start.3 = (bf16[1024,256]{1,0:T(8,128)(2,1)S(1)}, bf16[1024,256]{1,0:T(8,128)(2,1)}, u32[]{:S(2)}) copy-start(bf16[1024,256]{1,0:T(8,128)(2,1)} %all-reduce.2.cloned.1.call-done) | copy-start | bytes 1572868
  161.4 22.8 %copy-start.6 = (f32[16,16]{1,0:T(8,128)S(1)}, f32[16,16]{1,0:T(8,128)}, u32[]{:S(2)}) copy-start(f32[16,16]{1,0:T(8,128)} %param.10) | copy-start | bytes 3076
  182.4 1.0 copy-start.4
  194.0 8.3 %copy-start.5 = (bf16[512,256]{1,0:T(8,128)(2,1)S(1)}, bf16[512,256]{1,0:T(8,128)(2,1)}, u32[]{:S(2)}) copy-start(bf16[512,256]{1,0:T(8,128)(2,1)} %param.13) | copy-start | bytes 786436
  204.7 13.7 %all-to-all-start.1 = ((bf16[16,1,64,256]{3,2,1,0:T(8,128)(2,1)}), bf16[16,1,64,256]{3,2,1,0:T(8,128)(2,1)S(1)}, u32[]{:S(2)}, u32[]{:S(2)}) async-start(bf16[16,1,64,256]{3,2,1,0:T(8,128)(2,1)} %bitcast.64), calls=%async_computation.1 | async-start | bytes 1048576 | tf_op jit(solution)/shard_map/all_to_all | solution.py:79
  218.4 3.3 %copy-start.2 = (bf16[1,4096,256]{2,1,0:T(8,128)(2,1)S(1)}, bf16[1,4096,256]{2,1,0:T(8,128)(2,1)}, u32[]{:S(2)}) copy-start(bf16[1,4096,256]{2,1,0:T(8,128)(2,1)} %all-gather.3.cloned.1.call-done) | copy-start | bytes 6291460
Sparse Core Ops, SparseCore 0:
  9.8 42.6 all-gather.2
  59.1 93.1 all-reduce.1
where the time goes:
time: 238 us; the launch traced here: 237 us
  waiting for transfers between devices  146 us (61%)
  matrix products  27 us (11%)
  blocking collectives  19.4 us (8%)
  other arithmetic  16.5 us (7%)
  between operations  14.2 us (6%)
  local copies, waits for them, and re-layouts  9.15 us (4%)
  starting transfers between devices  4.91 us (2%)
    psum x1, waiting for transfers between devices, shards(): query = lax.psum(own, 'tm').astype(jnp.float32).astype(jnp.bfloat16)  93.3 us
    all_gather x1, waiting for transfers between devices, shards(): frame = lax.all_gather(tile, 'pts', axis=0, tiled=True)  43.1 us
    all_to_all x1, blocking collectives, shards(): lax.all_to_all(tokens, 'tm', split_axis=1, concat_axis=0, tiled=True)  19.4 us
    dot_general x4, matrix products, row_scores(): jnp.einsum('pc,jc->pj', rows, piece, preferred_element_type=jnp.float32)  9.02 us
    all_to_all x1, waiting for transfers between devices, shards(): lax.all_to_all(delta, 'tm', split_axis=0, concat_axis=1, tiled=True)  8.81 us
    dot_general x1, matrix products, mixer(): jnp.dot(upper, w_down, preferred_element_type=jnp.float32)  8.33 us
    reduce_sum x1, other arithmetic, shards(): parts_y.append(jnp.sum(expo * ys, axis=1) / total[:, 0])  5.97 us
    gather x1, local copies, waits for them, and re-layouts, shards(): picked = jnp.take(frame, query_pos, axis=0)  5.32 us
  transfers between devices with their start and end apart: 3, of which 3 were waited for; matrix products, arithmetic and copies ran while one was open for 1% of the time, Pallas kernels for 0%

commit v1 on v0

--- a/solution.py
+++ b/solution.py
@@ -31,13 +31,6 @@
     return delta.reshape(frames, count, w_query.shape[1])
 
 
-def grid_coords():
-    index = jnp.arange(HW, dtype=jnp.int32)
-    xs = (2 * (index % GRID) + 1).astype(jnp.float32) / GRID - 1.0
-    ys = (2 * (index // GRID) + 1).astype(jnp.float32) / GRID - 1.0
-    return (xs, ys)
-
-
 def row_scores(rows, piece, scale):
     return jnp.einsum("pc,jc->pj", rows, piece, preferred_element_type=jnp.float32) * scale
 
@@ -48,6 +41,38 @@
     return (expo, jnp.sum(expo, axis=1, keepdims=True))
 
 
+def ring_pairs(chips, step):
+    return [
+        (chip * 2 + core, (chip + step) % chips * 2 + core)
+        for chip in range(chips)
+        for core in range(2)
+    ]
+
+
+def swap_pairs(chips):
+    return [(chip * 2 + core, chip * 2 + 1 - core) for chip in range(chips) for core in range(2)]
+
+
+def gather_frame(tile, core):
+    chips = lax.axis_size("pts") // 2
+    swap = swap_pairs(chips)
+
+    def both(own):
+        other = lax.ppermute(own, "pts", swap)
+        even = core == 0
+        return [jnp.where(even, own, other), jnp.where(even, other, own)]
+
+    found = {0: both(tile)}
+    below = above = tile
+    for step in range(1, chips // 2 + 1):
+        below = lax.ppermute(below, "pts", ring_pairs(chips, 1))
+        if step < chips // 2:
+            above = lax.ppermute(above, "pts", ring_pairs(chips, -1))
+            found[step] = both(above)
+        found[chips - step] = both(below)
+    return jnp.concatenate([piece for at in range(chips) for piece in found[at]], axis=0)
+
+
 def shards(feats, query_frame, query_pos, time_mix, w_up, w_down, w_query):
     tile = feats[0]
     points = query_frame.shape[0]
@@ -55,29 +80,31 @@
     scale = width ** (-0.5)
     frame_id = lax.axis_index("tm")
     groups = lax.axis_size("tm")
-    xs, ys = grid_coords()
+    place = lax.axis_index("pts")
+    first_pos = place // 2 * 2 * tile.shape[0]
     block = min(512, points)
-    frame = lax.all_gather(tile, "pts", axis=0, tiled=True)
-    picked = jnp.take(frame, query_pos, axis=0)
+    frame = gather_frame(tile, place % 2)
+    index = (jnp.arange(HW, dtype=jnp.int32) + first_pos) % HW
+    xs = (2 * (index % GRID) + 1).astype(jnp.float32) / GRID - 1.0
+    ys = (2 * (index // GRID) + 1).astype(jnp.float32) / GRID - 1.0
+    picked = jnp.take(frame, (query_pos - first_pos) % HW, axis=0)
     own = jnp.where((query_frame == frame_id)[:, None], picked, jnp.zeros_like(picked))
-    query = lax.psum(own, "tm").astype(jnp.float32).astype(jnp.bfloat16)
+    share = points // groups
+    parts = lax.all_to_all(own.reshape(groups, share, width), "tm", 0, 0, tiled=True)
+    query_here = jnp.sum(parts.astype(jnp.float32), axis=0).astype(jnp.bfloat16)
+    query = lax.all_to_all(
+        jnp.broadcast_to(query_here, (groups, share, width)), "tm", 0, 0, tiled=True
+    ).reshape(points, width)
     pieces = []
     for first in range(0, points, block):
         expo, total = soft_parts(row_scores(query[first : first + block], frame, scale))
         product = jnp.dot(expo.astype(jnp.bfloat16), frame, preferred_element_type=jnp.float32)
         pieces.append((product / total).astype(jnp.bfloat16))
-    matched = jnp.concatenate(pieces, axis=0)
-    tokens = jnp.concatenate([matched, query], axis=1)
-    tokens = tokens.reshape(1, groups, points // groups, tokens.shape[1])
-    exchanged = lax.all_to_all(tokens, "tm", split_axis=1, concat_axis=0, tiled=True)
-    frames_here = exchanged.shape[0]
-    count = exchanged.shape[2]
-    result = mixer(
-        exchanged.reshape(frames_here, count, exchanged.shape[3]), time_mix, w_up, w_down, w_query
-    )
-    delta = result.reshape(frames_here, 1, count, result.shape[2])
-    returned = lax.all_to_all(delta, "tm", split_axis=0, concat_axis=1, tiled=True)
-    returned = returned.reshape(points, returned.shape[3])
+    matched = jnp.concatenate(pieces, axis=0).reshape(groups, share, width)
+    matched = lax.all_to_all(matched, "tm", 0, 0, tiled=True)
+    tokens = jnp.concatenate([matched, jnp.broadcast_to(query_here, matched.shape)], axis=2)
+    delta = mixer(tokens, time_mix, w_up, w_down, w_query)
+    returned = lax.all_to_all(delta, "tm", 0, 0, tiled=True).reshape(points, width)
     refined = (query.astype(jnp.float32) + returned.astype(jnp.float32)).astype(jnp.bfloat16)
     parts_x = []
     parts_y = []

time: 238 us -> 156 us (0.66)
  waiting for transfers between devices: 146 us -> 19.7 us
  blocking collectives: 19.4 us -> 45.6 us
  starting transfers between devices: 4.91 us -> 19.2 us
  between operations: 14.2 us -> 0.83 us
  other arithmetic: 16.5 us -> 28.7 us
  matrix products: 27 us -> 31.6 us
    psum x1 -> x0, waiting for transfers between devices: 93.3 us -> none  [shards(): query = lax.psum(own, 'tm').astype(jnp.float32).astype(jnp.bfloat16)]
    all_gather x1 -> x0, waiting for transfers between devices: 43.1 us -> none  [shards(): frame = lax.all_gather(tile, 'pts', axis=0, tiled=True)]
    all_to_all x1 -> x3, blocking collectives: 19.4 us -> 45.6 us  [the longest x1 18 us: shards(): lax.all_to_all(own.reshape(groups, share, width), 'tm', 0, 0, tiled=True)]
    ppermute x0 -> x15, starting transfers between devices: none -> 14.4 us  [the longest x3 12.9 us: gather_frame(): above = lax.ppermute(above, 'pts', ring_pairs(chips, -1))]
    unnamed x0 -> x15, other arithmetic: none -> 12 us
    ppermute x0 -> x15, waiting for transfers between devices: none -> 10.9 us  [the longest x4 9.45 us: gather_frame(): below = lax.ppermute(below, 'pts', ring_pairs(chips, 1))]
    dot_general x2, matrix products: 2.95 us -> 6.19 us  [shards(): jnp.dot(expo.astype(jnp.bfloat16), frame, preferred_element_type=jnp.floa...]
    dot_general x4, matrix products: 9.02 us -> 11.9 us  [row_scores(): jnp.einsum('pc,jc->pj', rows, piece, preferred_element_type=jnp.float32)]
  transfers between devices with their start and end apart: 3 -> 16, of which waited for: 3 -> 4; matrix products, arithmetic and copies ran while one was open for 1% -> 9% of each run, Pallas kernels for 0% -> 0%
where the time goes in v1:
time: 156 us; the launch traced here: 155 us
  blocking collectives  45.6 us (29%)
  matrix products  31.6 us (20%)
  other arithmetic  28.7 us (18%)
  waiting for transfers between devices  19.7 us (13%)
  starting transfers between devices  19.2 us (12%)
  local copies, waits for them, and re-layouts  9.59 us (6%)
    all_to_all x1, blocking collectives, shards(): lax.all_to_all(own.reshape(groups, share, width), 'tm', 0, 0, tiled=True)  18 us
    all_to_all x1, blocking collectives, shards(): lax.all_to_all(jnp.broadcast_to(query_here, (groups, share, width)), 'tm'...  14.3 us
    all_to_all x1, blocking collectives, shards(): matched = lax.all_to_all(matched, 'tm', 0, 0, tiled=True)  13.3 us
    ppermute x3, starting transfers between devices, gather_frame(): above = lax.ppermute(above, 'pts', ring_pairs(chips, -1))  12.9 us
    unnamed x15, other arithmetic  12 us
    dot_general x4, matrix products, row_scores(): jnp.einsum('pc,jc->pj', rows, piece, preferred_element_type=jnp.float32)  11.9 us
    ppermute x4, waiting for transfers between devices, gather_frame(): below = lax.ppermute(below, 'pts', ring_pairs(chips, 1))  9.45 us
    all_to_all x1, waiting for transfers between devices, shards(): lax.all_to_all(delta, 'tm', 0, 0, tiled=True).reshape(points, width)  8.79 us
  transfers between devices with their start and end apart: 16, of which 4 were waited for; matrix products, arithmetic and copies ran while one was open for 9% of the time, Pallas kernels for 0%

profile of v1, /device:TPU:8, one launch (start us, length us, event | category | flops | bytes accessed | tf_op | source)
XLA Modules:
  0.0 155.3 jit_solution(9678758581845198659)
XLA Ops:
  0.7 5.9 %collective-permute-start.1 = (bf16[256,256]{1,0:T(8,128)(2,1)}, bf16[256,256]{1,0:T(8,128)(2,1)S(1)}, u32[]{:S(2)}, u32[]{:S(2)}) collective-permute-start(bf16[256,256]{1,0:T(8,128)(2,1)} %bitcast.51), channel_id=1, source_target_pairs={{0,14},{1,15},{2,0},{3,1},{4,2},{5,3},{6,4},{7,5},{8,6},{9,7},{10,... | collective-permute-start | bytes 393224 | tf_op jit(solution)/shard_map/ppermute | solution.py:70
  10.4 3.6 %collective-permute-start.3 = (bf16[256,256]{1,0:T(8,128)(2,1)S(1)}, bf16[256,256]{1,0:T(8,128)(2,1)S(1)}, u32[]{:S(2)}, u32[]{:S(2)}) collective-permute-start(bf16[256,256]{1,0:T(8,128)(2,1)S(1)} %collective-permute-done.1), channel_id=1, source_target_pairs={{0,14},{1,15},{2,0},{3,1},{4,2},{5,3},{6,4},{7,5},{8,6},{9,7},{10,... | collective-permute-start | bytes 393224 | tf_op jit(solution)/shard_map/ppermute | solution.py:70
  14.2 1.6 %select_dynamic-update-slice_fusion.15 = bf16[4096,256]{1,0:T(8,128)(2,1)} fusion(bf16[256,256]{1,0:T(8,128)(2,1)S(1)} %collective-permute-done, pred[]{:T(512)S(6)} %eq.15, bf16[1,256,256]{2,1,0:T(8,128)(2,1)} %param.7), kind=kLoop, calls=%fused_computation.73 | loop fusion | flops 65535 | bytes 393217
  17.6 3.4 %collective-permute-start.5 = (bf16[256,256]{1,0:T(8,128)(2,1)S(1)}, bf16[256,256]{1,0:T(8,128)(2,1)S(1)}, u32[]{:S(2)}, u32[]{:S(2)}) collective-permute-start(bf16[256,256]{1,0:T(8,128)(2,1)S(1)} %collective-permute-done.3), channel_id=1, source_target_pairs={{0,14},{1,15},{2,0},{3,1},{4,2},{5,3},{6,4},{7,5},{8,6},{9,7},{10,... | collective-permute-start | bytes 393224 | tf_op jit(solution)/shard_map/ppermute | solution.py:70
  22.8 5.1 %collective-permute-done.9 = bf16[256,256]{1,0:T(8,128)(2,1)S(1)} collective-permute-done((bf16[256,256]{1,0:T(8,128)(2,1)S(1)}, bf16[256,256]{1,0:T(8,128)(2,1)S(1)}, u32[]{:S(2)}, u32[]{:S(2)}) %collective-permute-start.9) | collective-permute-done | bytes 131104 | tf_op jit(solution)/shard_map/ppermute | solution.py:68
  29.8 4.3 %collective-permute-done.10 = bf16[256,256]{1,0:T(8,128)(2,1)S(1)} collective-permute-done((bf16[256,256]{1,0:T(8,128)(2,1)S(1)}, bf16[256,256]{1,0:T(8,128)(2,1)S(1)}, u32[]{:S(2)}, u32[]{:S(2)}) %collective-permute-start.10) | collective-permute-done | bytes 131104 | tf_op jit(solution)/shard_map/ppermute | solution.py:68
  40.9 5.3 %gather_fusion = bf16[1024,256]{1,0:T(8,128)(2,1)S(1)} fusion(bf16[4096,256]{1,0:T(8,128)(2,1)} %select_dynamic-update-slice_fusion, s32[1024]{0:T(1024)S(1)} %broadcast_clamp_fusion), kind=kCustom, calls=%fused_computation | custom fusion | bytes 1052672 | tf_op jit(solution)/shard_map/jit(_take)/gather | solution.py:90
  46.6 18.0 %all_to_all.20 = bf16[16,64,256]{2,1,0:T(8,128)(2,1)S(1)} all-to-all(bf16[16,64,256]{2,1,0:T(8,128)(2,1)S(1)} %select_select_fusion), channel_id=1, replica_groups=mesh['tm'=16,'pts'=16] {'tm'}, dimensions={0} | all-to-all | bytes 1048576 | tf_op jit(solution)/shard_map/all_to_all | solution.py:93
  64.7 14.3 %all_to_all.21 = bf16[16,64,256]{2,1,0:T(8,128)(2,1)S(1)} all-to-all(bf16[16,64,256]{2,1,0:T(8,128)(2,1)S(1)} %broadcast_in_dim.57.clone), channel_id=1, replica_groups=mesh['tm'=16,'pts'=16] {'tm'}, dimensions={0} | all-to-all | bytes 1048576 | tf_op jit(solution)/shard_map/all_to_all | solution.py:95
  79.1 3.0 %multiply_reduce_fusion.7 = (f32[512]{0:T(512)S(1)}, f32[512,4096]{1,0:T(8,128)S(1)}) fusion(bf16[512,256]{1,0:T(8,128)(2,1)S(1)} %bitcast.49, bf16[4096,256]{1,0:T(8,128)(2,1)} %select_dynamic-update-slice_fusion), kind=kOutput, calls=%fused_computation.21 | convolution fusion | flops 1077935616 | bytes 10749952 | tf_op jit(solution)/shard_map/pc,jc->pj/dot_general | solution.py:35
  83.5 3.1 %fusion.37 = bf16[512,256]{1,0:T(8,128)(2,1)S(1)} fusion(bf16[4096,256]{1,0:T(8,128)(2,1)} %select_dynamic-update-slice_fusion, f32[512,4096]{1,0:T(8,128)S(1)} %get-tuple-element.22, f32[512]{0:T(512)S(1)} %get-tuple-element.21, f32[512]{0:T(512)S(1)} %fusion.8), kind=kOutput, calls=%fused_computation.50 | convolution fusion | flops 1080295424 | bytes 10752000 | tf_op jit(solution)/shard_map/dot_general | solution.py:101
  86.6 3.0 %multiply_reduce_fusion.6 = (f32[512]{0:T(512)S(1)}, f32[512,4096]{1,0:T(8,128)S(1)}) fusion(bf16[512,256]{1,0:T(8,128)(2,1)S(1)} %bitcast.46, bf16[4096,256]{1,0:T(8,128)(2,1)} %select_dynamic-update-slice_fusion), kind=kOutput, calls=%fused_computation.20 | convolution fusion | flops 1077935616 | bytes 10749952 | tf_op jit(solution)/shard_map/pc,jc->pj/dot_general | solution.py:35
  91.1 3.1 %fusion.43 = bf16[512,256]{1,0:T(8,128)(2,1)S(1)} fusion(bf16[4096,256]{1,0:T(8,128)(2,1)} %select_dynamic-update-slice_fusion, f32[512,4096]{1,0:T(8,128)S(1)} %get-tuple-element.20, f32[512]{0:T(512)S(1)} %get-tuple-element.19, f32[512]{0:T(512)S(1)} %fusion.10), kind=kOutput, calls=%fused_computation.52 | convolution fusion | flops 1080295424 | bytes 10752000 | tf_op jit(solution)/shard_map/dot_general | solution.py:101
  94.3 13.3 %all_to_all.22 = bf16[16,64,256]{2,1,0:T(8,128)(2,1)S(1)} all-to-all(bf16[16,64,256]{2,1,0:T(8,128)(2,1)S(1)} %bitcast.44), channel_id=1, replica_groups=mesh['tm'=16,'pts'=16] {'tm'}, dimensions={0} | all-to-all | bytes 1048576 | tf_op jit(solution)/shard_map/all_to_all | solution.py:104
  109.2 2.8 %multiply_reduce_fusion.8 = (f32[16,64]{0,1:T(8,128)S(1)}, f32[16,64,512]{2,0,1:T(8,128)S(1)}) fusion(f32[16,16]{1,0:T(8,128)S(1)} %copy-done.3, f32[16,64]{0,1:T(8,128)S(1)} %copy.25, bf16[16,64,256]{2,0,1:T(8,128)(2,1)} %copy-done.1, bf16[16,64,256]{2,0,1:T(8,128)(2,1)S(1)} %copy.23), kind=kOutput, calls=%fused_computation.45 | convolution fusion | flops 108526592 | bytes 3154944 | tf_op jit(solution)/shard_map/fg,gkd->fkd/dot_general | solution.py:18
  112.0 2.6 %copy.26 = f32[16,64,512]{2,1,0:T(8,128)} copy(f32[16,64,512]{2,0,1:T(8,128)S(1)} %get-tuple-element.24) | data formatting | bytes 4194304 | tf_op jit(solution)/shard_map/convert_element_type | solution.py:28
  114.7 2.8 %fusion.27 = bf16[1024,512]{1,0:T(8,128)(2,1)} fusion(f32[16,64,512]{2,1,0:T(8,128)} %copy.26, f32[1024]{0:T(1024)S(1)} %rsqrt.21), kind=kLoop, calls=%fused_computation.43 | loop fusion | flops 1048576 | bytes 3149824 | tf_op jit(solution)/shard_map/convert_element_type | solution.py:23
  117.5 8.3 %fusion.28 = bf16[1024,512]{1,0:T(8,128)(2,1)} fusion(f32[16,64,512]{2,1,0:T(8,128)} %copy.26, bf16[2048,512]{1,0:T(8,128)(2,1)S(1)} %copy-done, bf16[1024,512]{1,0:T(8,128)(2,1)} %fusion.27, bf16[512,2048]{1,0:T(8,128)(2,1)} %param.11), kind=kOutput, calls=%fused_computation.44 | convolution fusion | flops 4314890240 | bytes 8388608 | tf_op jit(solution)/shard_map/dot_general | solution.py:28
  125.8 2.4 %convolution_convert_fusion = bf16[1024,256]{1,0:T(8,128)(2,1)} fusion(bf16[1024,512]{1,0:T(8,128)(2,1)} %fusion.28, bf16[512,256]{1,0:T(8,128)(2,1)S(1)} %copy-done.2), kind=kOutput, calls=%fused_computation.48 | convolution fusion | flops 268697600 | bytes 1835008 | tf_op jit(solution)/shard_map/dot_general | solution.py:30
  128.3 4.8 %all-to-all-start.3 = ((bf16[16,64,256]{2,1,0:T(8,128)(2,1)}), bf16[16,64,256]{2,1,0:T(8,128)(2,1)S(1)}, u32[]{:S(2)}, u32[]{:S(2)}) async-start(bf16[16,64,256]{2,1,0:T(8,128)(2,1)} %bitcast.43), calls=%async_computation.3 | async-start | bytes 1048576 | tf_op jit(solution)/shard_map/all_to_all | solution.py:107
  133.2 8.8 %all-to-all-done.3 = bf16[16,64,256]{2,1,0:T(8,128)(2,1)S(1)} async-done(((bf16[16,64,256]{2,1,0:T(8,128)(2,1)}), bf16[16,64,256]{2,1,0:T(8,128)(2,1)S(1)}, u32[]{:S(2)}, u32[]{:S(2)}) %all-to-all-start.3) | async-done | bytes 524320 | tf_op jit(solution)/shard_map/all_to_all | solution.py:107
  142.2 3.0 %multiply_reduce_fusion.5 = (f32[512]{0:T(512)S(1)}, f32[512,4096]{1,0:T(8,128)S(1)}) fusion(bf16[512,256]{1,0:T(8,128)(2,1)S(1)} %bitcast.48, bf16[4096,256]{1,0:T(8,128)(2,1)} %select_dynamic-update-slice_fusion), kind=kOutput, calls=%fused_computation.19 | convolution fusion | flops 1077935616 | bytes 10749952 | tf_op jit(solution)/shard_map/pc,jc->pj/dot_general | solution.py:35
  145.1 3.0 %multiply_reduce_fusion.4 = (f32[512]{0:T(512)S(1)}, f32[512,4096]{1,0:T(8,128)S(1)}) fusion(bf16[512,256]{1,0:T(8,128)(2,1)S(1)} %bitcast.47, bf16[4096,256]{1,0:T(8,128)(2,1)} %select_dynamic-update-slice_fusion), kind=kOutput, calls=%fused_computation.18 | convolution fusion | flops 1077935616 | bytes 10749952 | tf_op jit(solution)/shard_map/pc,jc->pj/dot_general | solution.py:35
  148.1 6.0 %multiply_reduce_fusion = (f32[512]{0:T(512)S(1)}, f32[512]{0:T(512)S(1)}, f32[512]{0:T(512)S(1)}, f32[512]{0:T(512)S(1)}, f32[512]{0:T(512)S(1)}, /*index=5*/f32[512]{0:T(512)S(1)}) fusion(f32[512,4096]{1,0:T(8,128)S(1)} %get-tuple-element.26, f32[4096]{0:T(1024)S(1)} %get-tuple-element.30, f32[512]{0:T(512)S(1)} %get-tuple-element.25, ...), kind=kLoop, calls=%fused_computation.10 | loop fusion | flops 29357056 | bytes 16826368 | tf_op jit(solution)/shard_map/reduce_sum | solution.py:114
  (76 shorter events, 22.9 us)
Async XLA Ops:
  0.6 116.9 %copy-start = (bf16[2048,512]{1,0:T(8,128)(2,1)S(1)}, bf16[2048,512]{1,0:T(8,128)(2,1)}, u32[]{:S(2)}) copy-start(bf16[2048,512]{1,0:T(8,128)(2,1)} %param.12) | copy-start | bytes 6291460
  0.6 13.5 %collective-permute-start = (bf16[256,256]{1,0:T(8,128)(2,1)}, bf16[256,256]{1,0:T(8,128)(2,1)S(1)}, u32[]{:S(2)}, u32[]{:S(2)}) collective-permute-start(bf16[256,256]{1,0:T(8,128)(2,1)} %bitcast.50), channel_id=1, source_target_pairs={{0,1},{1,0},{2,3},{3,2},{4,5},{5,4},{6,7},{7,6},{8,9},{9,8},{10,11... | collective-permute-start | bytes 393224 | tf_op jit(solution)/shard_map/ppermute | solution.py:61
  0.7 9.6 %collective-permute-start.1 = (bf16[256,256]{1,0:T(8,128)(2,1)}, bf16[256,256]{1,0:T(8,128)(2,1)S(1)}, u32[]{:S(2)}, u32[]{:S(2)}) collective-permute-start(bf16[256,256]{1,0:T(8,128)(2,1)} %bitcast.51), channel_id=1, source_target_pairs={{0,14},{1,15},{2,0},{3,1},{4,2},{5,3},{6,4},{7,5},{8,6},{9,7},{10,... | collective-permute-start | bytes 393224 | tf_op jit(solution)/shard_map/ppermute | solution.py:70
  6.7 7.3 %collective-permute-start.7 = (bf16[256,256]{1,0:T(8,128)(2,1)}, bf16[256,256]{1,0:T(8,128)(2,1)S(1)}, u32[]{:S(2)}, u32[]{:S(2)}) collective-permute-start(bf16[256,256]{1,0:T(8,128)(2,1)} %bitcast.52), channel_id=1, source_target_pairs={{0,2},{1,3},{2,4},{3,5},{4,6},{5,7},{6,8},{7,9},{8,10},{9,11},{10,... | collective-permute-start | bytes 393224 | tf_op jit(solution)/shard_map/ppermute | solution.py:68
  10.3 10.7 %collective-permute-start.2 = (bf16[256,256]{1,0:T(8,128)(2,1)S(1)}, bf16[256,256]{1,0:T(8,128)(2,1)S(1)}, u32[]{:S(2)}, u32[]{:S(2)}) collective-permute-start(bf16[256,256]{1,0:T(8,128)(2,1)S(1)} %collective-permute-done.1), channel_id=1, source_target_pairs={{0,1},{1,0},{2,3},{3,2},{4,5},{5,4},{6,7},{7,6},{8,9},{9,8},{10,11... | collective-permute-start | bytes 393224 | tf_op jit(solution)/shard_map/ppermute | solution.py:61
  10.4 7.0 %collective-permute-start.3 = (bf16[256,256]{1,0:T(8,128)(2,1)S(1)}, bf16[256,256]{1,0:T(8,128)(2,1)S(1)}, u32[]{:S(2)}, u32[]{:S(2)}) collective-permute-start(bf16[256,256]{1,0:T(8,128)(2,1)S(1)} %collective-permute-done.1), channel_id=1, source_target_pairs={{0,14},{1,15},{2,0},{3,1},{4,2},{5,3},{6,4},{7,5},{8,6},{9,7},{10,... | collective-permute-start | bytes 393224 | tf_op jit(solution)/shard_map/ppermute | solution.py:70
  13.9 7.1 %collective-permute-start.8 = (bf16[256,256]{1,0:T(8,128)(2,1)S(1)}, bf16[256,256]{1,0:T(8,128)(2,1)S(1)}, u32[]{:S(2)}, u32[]{:S(2)}) collective-permute-start(bf16[256,256]{1,0:T(8,128)(2,1)S(1)} %collective-permute-done.7), channel_id=1, source_target_pairs={{0,2},{1,3},{2,4},{3,5},{4,6},{5,7},{6,8},{7,9},{8,10},{9,11},{10,... | collective-permute-start | bytes 393224 | tf_op jit(solution)/shard_map/ppermute | solution.py:68
  13.9 25.6 %collective-permute-start.14 = (bf16[256,256]{1,0:T(8,128)(2,1)S(1)}, bf16[256,256]{1,0:T(8,128)(2,1)S(1)}, u32[]{:S(2)}, u32[]{:S(2)}) collective-permute-start(bf16[256,256]{1,0:T(8,128)(2,1)S(1)} %collective-permute-done.7), channel_id=1, source_target_pairs={{0,1},{1,0},{2,3},{3,2},{4,5},{5,4},{6,7},{7,6},{8,9},{9,8},{10,11... | collective-permute-start | bytes 393224 | tf_op jit(solution)/shard_map/ppermute | solution.py:61
  17.4 10.5 %collective-permute-start.4 = (bf16[256,256]{1,0:T(8,128)(2,1)S(1)}, bf16[256,256]{1,0:T(8,128)(2,1)S(1)}, u32[]{:S(2)}, u32[]{:S(2)}) collective-permute-start(bf16[256,256]{1,0:T(8,128)(2,1)S(1)} %collective-permute-done.3), channel_id=1, source_target_pairs={{0,1},{1,0},{2,3},{3,2},{4,5},{5,4},{6,7},{7,6},{8,9},{9,8},{10,11... | collective-permute-start | bytes 393224 | tf_op jit(solution)/shard_map/ppermute | solution.py:61
  17.6 10.3 %collective-permute-start.5 = (bf16[256,256]{1,0:T(8,128)(2,1)S(1)}, bf16[256,256]{1,0:T(8,128)(2,1)S(1)}, u32[]{:S(2)}, u32[]{:S(2)}) collective-permute-start(bf16[256,256]{1,0:T(8,128)(2,1)S(1)} %collective-permute-done.3), channel_id=1, source_target_pairs={{0,14},{1,15},{2,0},{3,1},{4,2},{5,3},{6,4},{7,5},{8,6},{9,7},{10,... | collective-permute-start | bytes 393224 | tf_op jit(solution)/shard_map/ppermute | solution.py:70
  21.1 6.8 %collective-permute-start.9 = (bf16[256,256]{1,0:T(8,128)(2,1)S(1)}, bf16[256,256]{1,0:T(8,128)(2,1)S(1)}, u32[]{:S(2)}, u32[]{:S(2)}) collective-permute-start(bf16[256,256]{1,0:T(8,128)(2,1)S(1)} %collective-permute-done.8), channel_id=1, source_target_pairs={{0,2},{1,3},{2,4},{3,5},{4,6},{5,7},{6,8},{7,9},{8,10},{9,11},{10,... | collective-permute-start | bytes 393224 | tf_op jit(solution)/shard_map/ppermute | solution.py:68
  21.1 17.1 %collective-permute-start.13 = (bf16[256,256]{1,0:T(8,128)(2,1)S(1)}, bf16[256,256]{1,0:T(8,128)(2,1)S(1)}, u32[]{:S(2)}, u32[]{:S(2)}) collective-permute-start(bf16[256,256]{1,0:T(8,128)(2,1)S(1)} %collective-permute-done.8), channel_id=1, source_target_pairs={{0,1},{1,0},{2,3},{3,2},{4,5},{5,4},{6,7},{7,6},{8,9},{9,8},{10,11... | collective-permute-start | bytes 393224 | tf_op jit(solution)/shard_map/ppermute | solution.py:61
  27.9 6.2 %collective-permute-start.10 = (bf16[256,256]{1,0:T(8,128)(2,1)S(1)}, bf16[256,256]{1,0:T(8,128)(2,1)S(1)}, u32[]{:S(2)}, u32[]{:S(2)}) collective-permute-start(bf16[256,256]{1,0:T(8,128)(2,1)S(1)} %collective-permute-done.9), channel_id=1, source_target_pairs={{0,2},{1,3},{2,4},{3,5},{4,6},{5,7},{6,8},{7,9},{8,10},{9,11},{10,... | collective-permute-start | bytes 393224 | tf_op jit(solution)/shard_map/ppermute | solution.py:68
  27.9 8.9 %collective-permute-start.12 = (bf16[256,256]{1,0:T(8,128)(2,1)S(1)}, bf16[256,256]{1,0:T(8,128)(2,1)S(1)}, u32[]{:S(2)}, u32[]{:S(2)}) collective-permute-start(bf16[256,256]{1,0:T(8,128)(2,1)S(1)} %collective-permute-done.9), channel_id=1, source_target_pairs={{0,1},{1,0},{2,3},{3,2},{4,5},{5,4},{6,7},{7,6},{8,9},{9,8},{10,11... | collective-permute-start | bytes 393224 | tf_op jit(solution)/shard_map/ppermute | solution.py:61
  27.9 6.2 %collective-permute-start.6 = (bf16[256,256]{1,0:T(8,128)(2,1)S(1)}, bf16[256,256]{1,0:T(8,128)(2,1)S(1)}, u32[]{:S(2)}, u32[]{:S(2)}) collective-permute-start(bf16[256,256]{1,0:T(8,128)(2,1)S(1)} %collective-permute-done.5), channel_id=1, source_target_pairs={{0,1},{1,0},{2,3},{3,2},{4,5},{5,4},{6,7},{7,6},{8,9},{9,8},{10,11... | collective-permute-start | bytes 393224 | tf_op jit(solution)/shard_map/ppermute | solution.py:61
  34.1 1.4 collective-permute-start.11
  94.3 14.9 %copy-start.3 = (f32[16,16]{1,0:T(8,128)S(1)}, f32[16,16]{1,0:T(8,128)}, u32[]{:S(2)}) copy-start(f32[16,16]{1,0:T(8,128)} %param.10) | copy-start | bytes 3076
  108.0 0.8 copy-start.1
  117.5 8.3 %copy-start.2 = (bf16[512,256]{1,0:T(8,128)(2,1)S(1)}, bf16[512,256]{1,0:T(8,128)(2,1)}, u32[]{:S(2)}) copy-start(bf16[512,256]{1,0:T(8,128)(2,1)} %param.13) | copy-start | bytes 786436
  128.3 13.7 %all-to-all-start.3 = ((bf16[16,64,256]{2,1,0:T(8,128)(2,1)}), bf16[16,64,256]{2,1,0:T(8,128)(2,1)S(1)}, u32[]{:S(2)}, u32[]{:S(2)}) async-start(bf16[16,64,256]{2,1,0:T(8,128)(2,1)} %bitcast.43), calls=%async_computation.3 | async-start | bytes 1048576 | tf_op jit(solution)/shard_map/all_to_all | solution.py:107

commit v2 on v1

v2 whole, which is shorter than its diff:
```python
import functools

import jax
import jax.numpy as jnp
from jax import lax
from jax.experimental import pallas as pl
from jax.experimental.pallas import tpu as pltpu
from jax.sharding import PartitionSpec as P

GRID = 64
LOG2E=1.4426950408889634
VM=pl.BlockSpec(memory_space=pltpu.VMEM)
SM=pl.BlockSpec(memory_space=pltpu.SMEM)
NT=(((1,),(1,)),((),()))
def params(mb=40): return pltpu.CompilerParams(vmem_limit_bytes=mb<<20)

def pick_kernel(n, bases_ref, want_ref, *refs):
    tiles, out = refs[:n], refs[n]
    want = want_ref[...]
    acc = None
    for t in range(n):
        rows = tiles[t].shape[0]
        rel = want - bases_ref[t]
        hot = (rel == lax.broadcasted_iota(jnp.int32, (1, rows), 1)).astype(jnp.float32).astype(jnp.bfloat16)
        part = jnp.dot(hot, tiles[t][...], preferred_element_type=jnp.float32)
        acc = part if acc is None else acc + part
    out[...] = acc.astype(jnp.bfloat16)
def pick(bases, want, tiles):
    n=len(tiles)
    return pl.pallas_call(functools.partial(pick_kernel,n),
        out_shape=jax.ShapeDtypeStruct((want.shape[0],tiles[0].shape[1]),jnp.bfloat16),
        in_specs=[SM]+[VM]*(n+1), out_specs=VM, compiler_params=params())(bases,want,*tiles)

def match_kernel(n, bp, k, q_ref, *refs):
    tiles, out, bufs = refs[:n], refs[n], refs[n+1:]
    w = tiles[0].shape[0]
    blocks = q_ref.shape[0]//bp
    def score(i, t, m):
        s = lax.dot_general(q_ref[i*bp:(i+1)*bp], tiles[t][...], NT, preferred_element_type=jnp.float32)
        bufs[i%2][:, t*w:(t+1)*w] = s
        for h in range(0,w,128):
            m = s[:,h:h+128] if m is None else jnp.maximum(m, s[:,h:h+128])
        return m
    m=None
    for t in range(n): m=score(0,t,m)
    for i in range(blocks):
        top = jnp.max(m,axis=1,keepdims=True)*k
        m=None; acc=None; tot=None
        for t in range(n):
            if i+1<blocks: m=score(i+1,t,m)
            e = jnp.exp2(bufs[i%2][:, t*w:(t+1)*w]*k - top)
            for h in range(0,w,128):
                tot = e[:,h:h+128] if tot is None else tot+e[:,h:h+128]
            p = jnp.dot(e.astype(jnp.bfloat16), tiles[t][...], preferred_element_type=jnp.float32)
            acc = p if acc is None else acc+p
        total = jnp.sum(tot,axis=1,keepdims=True)
        out[i*bp:(i+1)*bp] = (acc/total).astype(jnp.bfloat16)
def match(q, tiles, bp=256):
    n=len(tiles); k=LOG2E*q.shape[1]**-0.5
    return pl.pallas_call(functools.partial(match_kernel,n,bp,k),
        out_shape=jax.ShapeDtypeStruct(q.shape,jnp.bfloat16),
        in_specs=[VM]*(n+1), out_specs=VM,
        scratch_shapes=[pltpu.VMEM((bp,n*tiles[0].shape[0]),jnp.float32)]*2, compiler_params=params())(q,*tiles)

def rematch_kernel(n, bp, k, grid, bases_ref, q_ref, *refs):
    tiles, ox, oy, bufs = refs[:n], refs[n], refs[n+1], refs[n+2:]
    w = tiles[0].shape[0]
    blocks = q_ref.shape[0]//bp
    lines = w//grid
    def score(i, t, m):
        s = lax.dot_general(tiles[t][...], q_ref[i*bp:(i+1)*bp], NT, preferred_element_type=jnp.float32)
        bufs[i%2][t*w:(t+1)*w] = s
        p = jnp.max(s.reshape(w//8,8,bp),axis=0)
        return p if m is None else jnp.maximum(m,p)
    xs = (2*lax.broadcasted_iota(jnp.int32,(grid,1),0)+1).astype(jnp.float32)/grid-1.0
    m=None
    for t in range(n): m=score(0,t,m)
    for i in range(blocks):
        top = jnp.max(m,axis=0,keepdims=True)*k
        m=None; cols=None; ysum=None
        for t in range(n):
            if i+1<blocks: m=score(i+1,t,m)
            line0 = bases_ref[t]//grid
            for r in range(lines):
                e = jnp.exp2(bufs[i%2][t*w+r*grid:t*w+(r+1)*grid]*k - top)
                cols = e if cols is None else cols+e
                y = (2*(line0+r)+1).astype(jnp.float32)/grid-1.0
                part = jnp.sum(e.reshape(grid//8,8,bp),axis=0)*y
                ysum = part if ysum is None else ysum+part
        total = jnp.sum(cols,axis=0,keepdims=True)
        ox[:,i*bp:(i+1)*bp] = jnp.sum(cols*xs,axis=0,keepdims=True)/total
        oy[:,i*bp:(i+1)*bp] = jnp.sum(ysum,axis=0,keepdims=True)/total
def rematch(bases, q, tiles, grid=64, bp=256):
    n=len(tiles); k=LOG2E*q.shape[1]**-0.5
    return pl.pallas_call(functools.partial(rematch_kernel,n,bp,k,grid),
        out_shape=[jax.ShapeDtypeStruct((1,q.shape[0]),jnp.float32)]*2,
        in_specs=[SM]+[VM]*(n+1), out_specs=[VM]*2,
        scratch_shapes=[pltpu.VMEM((n*tiles[0].shape[0],bp),jnp.float32)]*2, compiler_params=params())(bases,q,*tiles)

def prep_kernel(tm_ref, wd_ref, wq_ref, big_ref, fold_ref):
    f = tm_ref.shape[0]
    side = big_ref.shape[1]
    rep = side//f
    spread = (lax.broadcasted_iota(jnp.int32,(side,f),0)//rep == lax.broadcasted_iota(jnp.int32,(side,f),1)).astype(jnp.float32).astype(jnp.bfloat16)
    same = lax.broadcasted_iota(jnp.int32,(side,side),0)%rep == lax.broadcasted_iota(jnp.int32,(side,side),1)%rep
    rest = tm_ref[...]
    for part in range(big_ref.shape[0]):
        now = rest.astype(jnp.bfloat16)
        rest = rest - now.astype(jnp.float32)
        rows = jnp.dot(spread, now, preferred_element_type=jnp.float32).astype(jnp.bfloat16)
        full = lax.dot_general(rows, spread, NT, preferred_element_type=jnp.float32)
        big_ref[part] = jnp.where(same, full, 0.0).astype(jnp.bfloat16)
    fold_ref[...] = jnp.dot(wd_ref[...], wq_ref[...], preferred_element_type=jnp.float32).astype(jnp.bfloat16)
def prep(time_mix, w_down, w_query, parts=2):
    return pl.pallas_call(prep_kernel,
        out_shape=[jax.ShapeDtypeStruct((parts,256,256),jnp.bfloat16), jax.ShapeDtypeStruct((w_down.shape[0],w_query.shape[1]),jnp.bfloat16)],
        in_specs=[VM]*3, out_specs=[VM]*2, compiler_params=params())(time_mix,w_down,w_query)

def mixer_kernel(hid, m_ref, q_ref, big_ref, up_ref, fold_ref, wq_ref, out_ref):
    frames, points, width = m_ref.shape
    side = big_ref.shape[1]
    rep = side//frames
    for j in range(points//rep):
        here = slice(j*rep,(j+1)*rep)
        q = q_ref[here]
        both = jnp.concatenate([jnp.concatenate([m_ref[f,here] for f in range(frames)],axis=0),
                                jnp.concatenate([q]*frames,axis=0)],axis=1).astype(jnp.float32)
        normed = (both*lax.rsqrt(jnp.mean(both*both,axis=1,keepdims=True)+1e-6)).astype(jnp.bfloat16)
        sec = both
        for part in range(big_ref.shape[0]):
            sec = sec + jnp.dot(big_ref[part], normed, preferred_element_type=jnp.float32)
        sec16 = sec.astype(jnp.bfloat16)
        sec = sec16.astype(jnp.float32)
        inner = (sec*lax.rsqrt(jnp.mean(sec*sec,axis=1,keepdims=True)+1e-6)).astype(jnp.bfloat16)
        acc = jnp.dot(sec16, wq_ref[...], preferred_element_type=jnp.float32)
        for h in range(0, up_ref.shape[1], hid):
            u = jnp.dot(inner, up_ref[:,h:h+hid], preferred_element_type=jnp.float32)
            u = jax.nn.gelu(u).astype(jnp.bfloat16)
            acc = acc + jnp.dot(u, fold_ref[h:h+hid], preferred_element_type=jnp.float32)
        delta = acc.astype(jnp.bfloat16).astype(jnp.float32)
        q32 = q.astype(jnp.float32)
        for f in range(frames):
            out_ref[f,here] = (q32 + delta[f*rep:(f+1)*rep]).astype(jnp.bfloat16)
def mixer(m, q, big, w_up, fold, w_query, hid=256):
    return pl.pallas_call(functools.partial(mixer_kernel,hid),
        out_shape=jax.ShapeDtypeStruct(m.shape,jnp.bfloat16),
        in_specs=[VM]*6, out_specs=VM, compiler_params=params())(m,q,big,w_up,fold,w_query)


def ring_pairs(chips, step):
    return [
        (chip * 2 + core, (chip + step) % chips * 2 + core)
        for chip in range(chips)
        for core in range(2)
    ]


def swap_pairs(chips):
    return [(chip * 2 + core, chip * 2 + 1 - core) for chip in range(chips) for core in range(2)]


def gather_tiles(tile):
    chips = lax.axis_size("pts") // 2
    swap = swap_pairs(chips)
    found = {0: [tile, lax.ppermute(tile, "pts", swap)]}
    below = above = tile
    for step in range(1, chips // 2 + 1):
        below = lax.ppermute(below, "pts", ring_pairs(chips, 1))
        if step < chips // 2:
            above = lax.ppermute(above, "pts", ring_pairs(chips, -1))
            found[step] = [above, lax.ppermute(above, "pts", swap)]
        found[chips - step] = [below, lax.ppermute(below, "pts", swap)]
    tiles = [piece for at in range(chips) for piece in found[at]]
    place = lax.axis_index("pts")
    chip = (place // 2 + jnp.arange(chips, dtype=jnp.int32)) % chips
    core = jnp.array([0, 1], jnp.int32)
    bases = (chip[:, None] * 2 + (core + place) % 2) * tile.shape[0]
    return (tiles, bases.reshape(-1))


def shards(feats, query_frame, query_pos, time_mix, w_up, w_down, w_query):
    tile = feats[0]
    points = query_frame.shape[0]
    width = tile.shape[1]
    frame_id = lax.axis_index("tm")
    groups = lax.axis_size("tm")
    share = points // groups
    tiles, bases = gather_tiles(tile)
    want = jnp.where(query_frame == frame_id, query_pos, -1).reshape(points, 1)
    own = pick(bases, want, tiles)
    parts = lax.all_to_all(own.reshape(groups, share, width), "tm", 0, 0, tiled=True)
    query_here = jnp.sum(parts.astype(jnp.float32), axis=0).astype(jnp.bfloat16)
    query = lax.all_to_all(
        jnp.broadcast_to(query_here, (groups, share, width)), "tm", 0, 0, tiled=True
    ).reshape(points, width)
    mixes, folded = prep(time_mix, w_down, w_query)
    matched = match(query, tiles).reshape(groups, share, width)
    matched = lax.all_to_all(matched, "tm", 0, 0, tiled=True)
    refined = mixer(matched, query_here, mixes, w_up, folded, w_query)
    refined = lax.all_to_all(refined, "tm", 0, 0, tiled=True).reshape(points, width)
    return rematch(bases, refined, tiles, GRID)


def solution(mesh):
    placed = (P("tm", "pts", None), P("pts"), P("pts"), P(), P(), P(), P())
    return jax.shard_map(
        shards,
        mesh=mesh,
        in_specs=placed,
        out_specs=(P("tm", "pts"), P("tm", "pts")),
        check_vma=False,
    )
```

time: 156 us -> 120 us (0.77)
  matrix products: 31.6 us -> 0 us
  other arithmetic: 28.7 us -> 0.92 us
  Pallas kernels: 0 us -> 26.2 us
  waiting for transfers between devices: 19.7 us -> 17.4 us
    dot_general x9 -> x0, matrix products: 31.6 us -> none  [the longest x4 11.9 us: row_scores(): jnp.einsum('pc,jc->pj', rows, piece, preferred_element_type=jnp.float32)]
    pallas_call x0 -> x5, Pallas kernels: none -> 26.2 us  [the longest x1 7.84 us: match(): pl.pallas_call(functools.partial(match_kernel, n, bp, k), out_shape=jax.S...]
    unnamed x15 -> x0, other arithmetic: 12 us -> none
    reduce_sum x4 -> x0, other arithmetic: 9.25 us -> none  [the longest x1 5.97 us: shards(): parts_y.append(jnp.sum(expo * ys, axis=1) / total[:, 0])]
    unnamed x8 -> x62, local copies, waits for them, and re-layouts: 0.81 us -> 9.13 us
    gather x1 -> x0, local copies, waits for them, and re-layouts: 5.32 us -> none  [shards(): picked = jnp.take(frame, (query_pos - first_pos) % HW, axis=0)]
    all_to_all x1, waiting for transfers between devices: 8.79 us -> 3.65 us  [shards(): matched = lax.all_to_all(matched, 'tm', 0, 0, tiled=True)]
    convert_element_type x2 -> x0, other arithmetic: 2.98 us -> none  [the longest x1 2.83 us: mixer(): inner = rms_rows(flat.astype(jnp.float32)).astype(jnp.bfloat16)]
  transfers between devices with their start and end apart: 16 -> 16, of which waited for: 4 -> 6; matrix products, arithmetic and copies ran while one was open for 9% -> 1% of each run, Pallas kernels for 0% -> 1%
where the time goes in v2:
time: 120 us
  blocking collectives  45.4 us (38%)
  Pallas kernels  26.2 us (22%)
  starting transfers between devices  19.4 us (16%)
  waiting for transfers between devices  17.4 us (14%)
  local copies, waits for them, and re-layouts  9.48 us (8%)
    all_to_all x1, blocking collectives, shards(): lax.all_to_all(own.reshape(groups, share, width), 'tm', 0, 0, tiled=True)  17.9 us
    all_to_all x1, blocking collectives, shards(): lax.all_to_all(jnp.broadcast_to(query_here, (groups, share, width)), 'tm'...  14.1 us
    ppermute x4, waiting for transfers between devices, gather_tiles(): below = lax.ppermute(below, 'pts', ring_pairs(chips, 1))  13.4 us
    all_to_all x1, blocking collectives, shards(): lax.all_to_all(refined, 'tm', 0, 0, tiled=True).reshape(points, width)  13.3 us
    ppermute x3, starting transfers between devices, gather_tiles(): above = lax.ppermute(above, 'pts', ring_pairs(chips, -1))  10.8 us
    unnamed x62, local copies, waits for them, and re-layouts  9.13 us
    pallas_call x1, Pallas kernels, match(): pl.pallas_call(functools.partial(match_kernel, n, bp, k), out_shape=jax.S...  7.84 us
    pallas_call x1, Pallas kernels, rematch(): pl.pallas_call(functools.partial(rematch_kernel, n, bp, k, grid), out_sha...  7.39 us
  transfers between devices with their start and end apart: 16, of which 6 were waited for; matrix products, arithmetic and copies ran while one was open for 1% of the time, Pallas kernels for 1%

profile of v2, /device:TPU:8, one launch (start us, length us, event | category | flops | bytes accessed | tf_op | source)
XLA Modules:
  0.0 119.9 jit_solution(16965187282116459891)
XLA Ops:
  0.6 2.0 %collective-permute-start.7 = (bf16[256,256]{1,0:T(8,128)(2,1)}, bf16[256,256]{1,0:T(8,128)(2,1)S(1)}, u32[]{:S(2)}, u32[]{:S(2)}) collective-permute-start(bf16[256,256]{1,0:T(8,128)(2,1)} %bitcast.9), channel_id=1, source_target_pairs={{0,2},{1,3},{2,4},{3,5},{4,6},{5,7},{6,8},{7,9},{8,10},{9,11},{10,... | collective-permute-start | bytes 393224 | tf_op jit(solution)/shard_map/ppermute | solution.py:168
  2.6 4.0 %collective-permute-start.1 = (bf16[256,256]{1,0:T(8,128)(2,1)}, bf16[256,256]{1,0:T(8,128)(2,1)S(1)}, u32[]{:S(2)}, u32[]{:S(2)}) collective-permute-start(bf16[256,256]{1,0:T(8,128)(2,1)} %bitcast.10), channel_id=1, source_target_pairs={{0,14},{1,15},{2,0},{3,1},{4,2},{5,3},{6,4},{7,5},{8,6},{9,7},{10,... | collective-permute-start | bytes 393224 | tf_op jit(solution)/shard_map/ppermute | solution.py:170
  6.7 3.6 %collective-permute-done.7.refs_14_ = bf16[256,256]{1,0:T(8,128)(2,1)S(1)} collective-permute-done((bf16[256,256]{1,0:T(8,128)(2,1)}, bf16[256,256]{1,0:T(8,128)(2,1)S(1)}, u32[]{:S(2)}, u32[]{:S(2)}) %collective-permute-start.7) | collective-permute-done | bytes 131104 | tf_op jit(solution)/shard_map/ppermute | solution.py:168
  10.3 3.2 %collective-permute-start.3 = (bf16[256,256]{1,0:T(8,128)(2,1)S(1)}, bf16[256,256]{1,0:T(8,128)(2,1)S(1)}, u32[]{:S(2)}, u32[]{:S(2)}) collective-permute-start(bf16[256,256]{1,0:T(8,128)(2,1)S(1)} %collective-permute-done.1.refs_2_), channel_id=1, source_target_pairs={{0,14},{1,15},{2,0},{3,1},{4,2},{5,3},{6,4},{7,5},{8,6},{9,7},{10,... | collective-permute-start | bytes 393224 | tf_op jit(solution)/shard_map/ppermute | solution.py:170
  13.5 2.9 %collective-permute-done.8.refs_12_ = bf16[256,256]{1,0:T(8,128)(2,1)S(1)} collective-permute-done((bf16[256,256]{1,0:T(8,128)(2,1)S(1)}, bf16[256,256]{1,0:T(8,128)(2,1)S(1)}, u32[]{:S(2)}, u32[]{:S(2)}) %collective-permute-start.8) | collective-permute-done | bytes 131104 | tf_op jit(solution)/shard_map/ppermute | solution.py:168
  17.1 3.5 %collective-permute-start.5 = (bf16[256,256]{1,0:T(8,128)(2,1)S(1)}, bf16[256,256]{1,0:T(8,128)(2,1)S(1)}, u32[]{:S(2)}, u32[]{:S(2)}) collective-permute-start(bf16[256,256]{1,0:T(8,128)(2,1)S(1)} %collective-permute-done.3.refs_4_), channel_id=1, source_target_pairs={{0,14},{1,15},{2,0},{3,1},{4,2},{5,3},{6,4},{7,5},{8,6},{9,7},{10,... | collective-permute-start | bytes 393224 | tf_op jit(solution)/shard_map/ppermute | solution.py:170
  20.6 2.0 %collective-permute-done.9.refs_10_ = bf16[256,256]{1,0:T(8,128)(2,1)S(1)} collective-permute-done((bf16[256,256]{1,0:T(8,128)(2,1)S(1)}, bf16[256,256]{1,0:T(8,128)(2,1)S(1)}, u32[]{:S(2)}, u32[]{:S(2)}) %collective-permute-start.9) | collective-permute-done | bytes 131104 | tf_op jit(solution)/shard_map/ppermute | solution.py:168
  23.9 4.9 %collective-permute-done.10.refs_8_ = bf16[256,256]{1,0:T(8,128)(2,1)S(1)} collective-permute-done((bf16[256,256]{1,0:T(8,128)(2,1)S(1)}, bf16[256,256]{1,0:T(8,128)(2,1)S(1)}, u32[]{:S(2)}, u32[]{:S(2)}) %collective-permute-start.10) | collective-permute-done | bytes 131104 | tf_op jit(solution)/shard_map/ppermute | solution.py:168
  30.2 0.9 copy-done.2
  31.1 3.9 %shard_map.95 = bf16[1024,256]{1,0:T(8,128)(2,1)S(1)} custom-call(s32[16]{0:T(128)S(1)} %mul.17.bases_ref, s32[1024,1]{1,0:T(8,128)S(1)} %copy.10.want_ref, bf16[256,256]{1,0:T(8,128)(2,1)S(1)} %bitcast.12, bf16[256,256]{1,0:T(8,128)(2,1)S(1)} %collective-permute-done.refs_1_, bf16[256,256]{1,0:T(8,128)(2,1)S(1)} %collective-permute-done.1.refs_2_, ...), custom_call_target="tpu_custom_call" | custom-call | tf_op jit(solution)/shard_map/pallas_call | solution.py:30
  35.0 17.9 %all_to_all.20 = bf16[16,64,256]{2,1,0:T(8,128)(2,1)S(1)} all-to-all(bf16[16,64,256]{2,1,0:T(8,128)(2,1)S(1)} %bitcast.7), channel_id=1, replica_groups=mesh['tm'=16,'pts'=16] {'tm'}, dimensions={0} | all-to-all | bytes 1048576 | tf_op jit(solution)/shard_map/all_to_all | solution.py:191
  53.0 14.1 %all_to_all.21 = bf16[16,64,256]{2,1,0:T(8,128)(2,1)S(1)} all-to-all(bf16[16,64,256]{2,1,0:T(8,128)(2,1)S(1)} %broadcast_in_dim.10), channel_id=1, replica_groups=mesh['tm'=16,'pts'=16] {'tm'}, dimensions={0} | all-to-all | bytes 1048576 | tf_op jit(solution)/shard_map/all_to_all | solution.py:193
  67.2 7.8 %shard_map.96 = bf16[1024,256]{1,0:T(8,128)(2,1)} custom-call(bf16[1024,256]{1,0:T(8,128)(2,1)S(1)} %bitcast.8, bf16[256,256]{1,0:T(8,128)(2,1)S(1)} %bitcast.13, bf16[256,256]{1,0:T(8,128)(2,1)S(1)} %collective-permute-done.refs_1_, bf16[256,256]{1,0:T(8,128)(2,1)S(1)} %collective-permute-done.1.refs_2_, ...), custom_call_target="tpu_custom_call" | custom-call | tf_op jit(solution)/shard_map/pallas_call | solution.py:60
  75.1 5.0 %all-to-all-start.2 = ((bf16[16,64,256]{2,1,0:T(8,128)(2,1)}), bf16[16,64,256]{2,1,0:T(8,128)(2,1)S(1)}, u32[]{:S(2)}, u32[]{:S(2)}) async-start(bf16[16,64,256]{2,1,0:T(8,128)(2,1)} %bitcast.4), calls=%async_computation.2 | async-start | bytes 1048576 | tf_op jit(solution)/shard_map/all_to_all | solution.py:198
  80.1 1.6 %copy-done.1 = bf16[2048,512]{1,0:T(8,128)(2,1)S(1)} copy-done((bf16[2048,512]{1,0:T(8,128)(2,1)S(1)}, bf16[2048,512]{1,0:T(8,128)(2,1)}, u32[]{:S(2)}) %copy-start.1) | copy-done | bytes 2097176
  81.6 0.9 copy-done.22
  83.5 1.0 copy-done.24
  85.2 3.6 %all-to-all-done.2.m_ref = bf16[16,64,256]{2,1,0:T(8,128)(2,1)S(1)} async-done(((bf16[16,64,256]{2,1,0:T(8,128)(2,1)}), bf16[16,64,256]{2,1,0:T(8,128)(2,1)S(1)}, u32[]{:S(2)}, u32[]{:S(2)}) %all-to-all-start.2) | async-done | bytes 524320 | tf_op jit(solution)/shard_map/all_to_all | solution.py:198
  88.9 0.9 copy-done.23
  89.8 1.2 %copy-done.25 = bf16[2048,256]{1,0:T(8,128)(2,1)S(1)} copy-done((bf16[2048,256]{1,0:T(8,128)(2,1)S(1)}, bf16[2048,256]{1,0:T(8,128)(2,1)}, u32[]{:S(2)}) %copy-start.25) | copy-done | bytes 1048600
  91.8 0.9 copy-done.29
  92.8 6.2 %shard_map.98 = bf16[16,64,256]{2,1,0:T(8,128)(2,1)S(1)} custom-call(bf16[16,64,256]{2,1,0:T(8,128)(2,1)S(1)} %all-to-all-done.2.m_ref, bf16[64,256]{1,0:T(8,128)(2,1)S(1)} %copy-done.27, bf16[2,256,256]{2,1,0:T(8,128)(2,1)S(1)} %copy-done.29, bf16[512,2048]{1,0:T(8,128)(2,1)S(1)} %copy-done, bf16[2048,256]{1,0:T(8,128)(2,1)S(1)} %copy-done.25, ...), custom_call_target="tpu_custom_call" | custom-call | tf_op jit(solution)/shard_map/pallas_call | solution.py:145
  99.0 13.3 %all_to_all.22 = bf16[16,64,256]{2,1,0:T(8,128)(2,1)S(1)} all-to-all(bf16[16,64,256]{2,1,0:T(8,128)(2,1)S(1)} %shard_map.98), channel_id=1, replica_groups=mesh['tm'=16,'pts'=16] {'tm'}, dimensions={0} | all-to-all | bytes 1048576 | tf_op jit(solution)/shard_map/all_to_all | solution.py:200
  112.5 7.4 %shard_map.99 = (f32[1,1024]{1,0:T(1,128)}, f32[1,1024]{1,0:T(1,128)}) custom-call(s32[16]{0:T(128)S(1)} %mul.17.bases_ref, bf16[1024,256]{1,0:T(8,128)(2,1)S(1)} %bitcast.6, bf16[256,256]{1,0:T(8,128)(2,1)S(1)} %bitcast.14, bf16[256,256]{1,0:T(8,128)(2,1)S(1)} %collective-permute-done.refs_1_, bf16[256,256]{1,0:T(8,128)(2,1)S(1)} %collective-permute-done.1.refs_2_, ...), custom_call_target="tpu_custom_call" | custom-call | tf_op jit(solution)/shard_map/pallas_call | solution.py:95
  (86 shorter events, 5.7 us)
Async XLA Ops:
  0.6 9.6 %collective-permute-start.7 = (bf16[256,256]{1,0:T(8,128)(2,1)}, bf16[256,256]{1,0:T(8,128)(2,1)S(1)}, u32[]{:S(2)}, u32[]{:S(2)}) collective-permute-start(bf16[256,256]{1,0:T(8,128)(2,1)} %bitcast.9), channel_id=1, source_target_pairs={{0,2},{1,3},{2,4},{3,5},{4,6},{5,7},{6,8},{7,9},{8,10},{9,11},{10,... | collective-permute-start | bytes 393224 | tf_op jit(solution)/shard_map/ppermute | solution.py:168
  2.6 7.7 %collective-permute-start.1 = (bf16[256,256]{1,0:T(8,128)(2,1)}, bf16[256,256]{1,0:T(8,128)(2,1)S(1)}, u32[]{:S(2)}, u32[]{:S(2)}) collective-permute-start(bf16[256,256]{1,0:T(8,128)(2,1)} %bitcast.10), channel_id=1, source_target_pairs={{0,14},{1,15},{2,0},{3,1},{4,2},{5,3},{6,4},{7,5},{8,6},{9,7},{10,... | collective-permute-start | bytes 393224 | tf_op jit(solution)/shard_map/ppermute | solution.py:170
  10.3 6.2 %collective-permute-start.8 = (bf16[256,256]{1,0:T(8,128)(2,1)S(1)}, bf16[256,256]{1,0:T(8,128)(2,1)S(1)}, u32[]{:S(2)}, u32[]{:S(2)}) collective-permute-start(bf16[256,256]{1,0:T(8,128)(2,1)S(1)} %collective-permute-done.7.refs_14_), channel_id=1, source_target_pairs={{0,2},{1,3},{2,4},{3,5},{4,6},{5,7},{6,8},{7,9},{8,10},{9,11},{10,... | collective-permute-start | bytes 393224 | tf_op jit(solution)/shard_map/ppermute | solution.py:168
  10.3 12.5 %collective-permute-start = (bf16[256,256]{1,0:T(8,128)(2,1)}, bf16[256,256]{1,0:T(8,128)(2,1)S(1)}, u32[]{:S(2)}, u32[]{:S(2)}) collective-permute-start(bf16[256,256]{1,0:T(8,128)(2,1)} %bitcast.11), channel_id=1, source_target_pairs={{0,1},{1,0},{2,3},{3,2},{4,5},{5,4},{6,7},{7,6},{8,9},{9,8},{10,11... | collective-permute-start | bytes 393224 | tf_op jit(solution)/shard_map/ppermute | solution.py:165
  10.3 6.8 %collective-permute-start.3 = (bf16[256,256]{1,0:T(8,128)(2,1)S(1)}, bf16[256,256]{1,0:T(8,128)(2,1)S(1)}, u32[]{:S(2)}, u32[]{:S(2)}) collective-permute-start(bf16[256,256]{1,0:T(8,128)(2,1)S(1)} %collective-permute-done.1.refs_2_), channel_id=1, source_target_pairs={{0,14},{1,15},{2,0},{3,1},{4,2},{5,3},{6,4},{7,5},{8,6},{9,7},{10,... | collective-permute-start | bytes 393224 | tf_op jit(solution)/shard_map/ppermute | solution.py:170
  16.4 6.2 %collective-permute-start.9 = (bf16[256,256]{1,0:T(8,128)(2,1)S(1)}, bf16[256,256]{1,0:T(8,128)(2,1)S(1)}, u32[]{:S(2)}, u32[]{:S(2)}) collective-permute-start(bf16[256,256]{1,0:T(8,128)(2,1)S(1)} %collective-permute-done.8.refs_12_), channel_id=1, source_target_pairs={{0,2},{1,3},{2,4},{3,5},{4,6},{5,7},{6,8},{7,9},{8,10},{9,11},{10,... | collective-permute-start | bytes 393224 | tf_op jit(solution)/shard_map/ppermute | solution.py:168
  16.5 6.4 %collective-permute-start.14 = (bf16[256,256]{1,0:T(8,128)(2,1)S(1)}, bf16[256,256]{1,0:T(8,128)(2,1)S(1)}, u32[]{:S(2)}, u32[]{:S(2)}) collective-permute-start(bf16[256,256]{1,0:T(8,128)(2,1)S(1)} %collective-permute-done.7.refs_14_), channel_id=1, source_target_pairs={{0,1},{1,0},{2,3},{3,2},{4,5},{5,4},{6,7},{7,6},{8,9},{9,8},{10,11... | collective-permute-start | bytes 393224 | tf_op jit(solution)/shard_map/ppermute | solution.py:172
  16.6 6.8 %collective-permute-start.2 = (bf16[256,256]{1,0:T(8,128)(2,1)S(1)}, bf16[256,256]{1,0:T(8,128)(2,1)S(1)}, u32[]{:S(2)}, u32[]{:S(2)}) collective-permute-start(bf16[256,256]{1,0:T(8,128)(2,1)S(1)} %collective-permute-done.1.refs_2_), channel_id=1, source_target_pairs={{0,1},{1,0},{2,3},{3,2},{4,5},{5,4},{6,7},{7,6},{8,9},{9,8},{10,11... | collective-permute-start | bytes 393224 | tf_op jit(solution)/shard_map/ppermute | solution.py:171
  17.1 6.4 %collective-permute-start.5 = (bf16[256,256]{1,0:T(8,128)(2,1)S(1)}, bf16[256,256]{1,0:T(8,128)(2,1)S(1)}, u32[]{:S(2)}, u32[]{:S(2)}) collective-permute-start(bf16[256,256]{1,0:T(8,128)(2,1)S(1)} %collective-permute-done.3.refs_4_), channel_id=1, source_target_pairs={{0,14},{1,15},{2,0},{3,1},{4,2},{5,3},{6,4},{7,5},{8,6},{9,7},{10,... | collective-permute-start | bytes 393224 | tf_op jit(solution)/shard_map/ppermute | solution.py:170
  22.6 6.2 %collective-permute-start.10 = (bf16[256,256]{1,0:T(8,128)(2,1)S(1)}, bf16[256,256]{1,0:T(8,128)(2,1)S(1)}, u32[]{:S(2)}, u32[]{:S(2)}) collective-permute-start(bf16[256,256]{1,0:T(8,128)(2,1)S(1)} %collective-permute-done.9.refs_10_), channel_id=1, source_target_pairs={{0,2},{1,3},{2,4},{3,5},{4,6},{5,7},{6,8},{7,9},{8,10},{9,11},{10,... | collective-permute-start | bytes 393224 | tf_op jit(solution)/shard_map/ppermute | solution.py:168
  22.8 7.0 %collective-permute-start.13 = (bf16[256,256]{1,0:T(8,128)(2,1)S(1)}, bf16[256,256]{1,0:T(8,128)(2,1)S(1)}, u32[]{:S(2)}, u32[]{:S(2)}) collective-permute-start(bf16[256,256]{1,0:T(8,128)(2,1)S(1)} %collective-permute-done.8.refs_12_), channel_id=1, source_target_pairs={{0,1},{1,0},{2,3},{3,2},{4,5},{5,4},{6,7},{7,6},{8,9},{9,8},{10,11... | collective-permute-start | bytes 393224 | tf_op jit(solution)/shard_map/ppermute | solution.py:172
  22.9 44.2 %copy-start.4 = (bf16[256,256]{1,0:T(8,128)(2,1)}, bf16[256,256]{1,0:T(8,128)(2,1)S(1)}, u32[]{:S(2)}) copy-start(bf16[256,256]{1,0:T(8,128)(2,1)S(1)} %collective-permute-done.14.refs_15_) | copy-start | bytes 393220
  22.9 6.9 %collective-permute-start.4 = (bf16[256,256]{1,0:T(8,128)(2,1)S(1)}, bf16[256,256]{1,0:T(8,128)(2,1)S(1)}, u32[]{:S(2)}, u32[]{:S(2)}) collective-permute-start(bf16[256,256]{1,0:T(8,128)(2,1)S(1)} %collective-permute-done.3.refs_4_), channel_id=1, source_target_pairs={{0,1},{1,0},{2,3},{3,2},{4,5},{5,4},{6,7},{7,6},{8,9},{9,8},{10,11... | collective-permute-start | bytes 393224 | tf_op jit(solution)/shard_map/ppermute | solution.py:171
  23.4 43.8 %copy-start.6 = (bf16[256,256]{1,0:T(8,128)(2,1)}, bf16[256,256]{1,0:T(8,128)(2,1)S(1)}, u32[]{:S(2)}) copy-start(bf16[256,256]{1,0:T(8,128)(2,1)S(1)} %collective-permute-done.2.refs_3_) | copy-start | bytes 393220
  23.4 6.4 %collective-permute-start.12 = (bf16[256,256]{1,0:T(8,128)(2,1)S(1)}, bf16[256,256]{1,0:T(8,128)(2,1)S(1)}, u32[]{:S(2)}, u32[]{:S(2)}) collective-permute-start(bf16[256,256]{1,0:T(8,128)(2,1)S(1)} %collective-permute-done.9.refs_10_), channel_id=1, source_target_pairs={{0,1},{1,0},{2,3},{3,2},{4,5},{5,4},{6,7},{7,6},{8,9},{9,8},{10,11... | collective-permute-start | bytes 393224 | tf_op jit(solution)/shard_map/ppermute | solution.py:172
  23.5 43.6 %copy-start.8 = (bf16[256,256]{1,0:T(8,128)(2,1)}, bf16[256,256]{1,0:T(8,128)(2,1)S(1)}, u32[]{:S(2)}) copy-start(bf16[256,256]{1,0:T(8,128)(2,1)S(1)} %collective-permute-done.5.refs_6_) | copy-start | bytes 393220
  23.5 6.3 %collective-permute-start.6 = (bf16[256,256]{1,0:T(8,128)(2,1)S(1)}, bf16[256,256]{1,0:T(8,128)(2,1)S(1)}, u32[]{:S(2)}, u32[]{:S(2)}) collective-permute-start(bf16[256,256]{1,0:T(8,128)(2,1)S(1)} %collective-permute-done.5.refs_6_), channel_id=1, source_target_pairs={{0,1},{1,0},{2,3},{3,2},{4,5},{5,4},{6,7},{7,6},{8,9},{9,8},{10,11... | collective-permute-start | bytes 393224 | tf_op jit(solution)/shard_map/ppermute | solution.py:171
  28.8 38.3 %copy-start.10 = (bf16[256,256]{1,0:T(8,128)(2,1)}, bf16[256,256]{1,0:T(8,128)(2,1)S(1)}, u32[]{:S(2)}) copy-start(bf16[256,256]{1,0:T(8,128)(2,1)S(1)} %collective-permute-done.10.refs_8_) | copy-start | bytes 393220
  28.8 1.3 %collective-permute-start.11 = (bf16[256,256]{1,0:T(8,128)(2,1)S(1)}, bf16[256,256]{1,0:T(8,128)(2,1)S(1)}, u32[]{:S(2)}, u32[]{:S(2)}) collective-permute-start(bf16[256,256]{1,0:T(8,128)(2,1)S(1)} %collective-permute-done.10.refs_8_), channel_id=1, source_target_pairs={{0,1},{1,0},{2,3},{3,2},{4,5},{5,4},{6,7},{7,6},{8,9},{9,8},{10,11... | collective-permute-start | bytes 393224 | tf_op jit(solution)/shard_map/ppermute | solution.py:172
  29.8 37.4 %copy-start.12 = (bf16[256,256]{1,0:T(8,128)(2,1)}, bf16[256,256]{1,0:T(8,128)(2,1)S(1)}, u32[]{:S(2)}) copy-start(bf16[256,256]{1,0:T(8,128)(2,1)S(1)} %collective-permute-done.13.refs_13_) | copy-start | bytes 393220
  29.8 37.3 %copy-start.14 = (bf16[256,256]{1,0:T(8,128)(2,1)}, bf16[256,256]{1,0:T(8,128)(2,1)S(1)}, u32[]{:S(2)}) copy-start(bf16[256,256]{1,0:T(8,128)(2,1)S(1)} %collective-permute-done.4.refs_5_) | copy-start | bytes 393220
  29.8 37.3 %copy-start.16 = (bf16[256,256]{1,0:T(8,128)(2,1)}, bf16[256,256]{1,0:T(8,128)(2,1)S(1)}, u32[]{:S(2)}) copy-start(bf16[256,256]{1,0:T(8,128)(2,1)S(1)} %collective-permute-done.12.refs_11_) | copy-start | bytes 393220
  29.9 37.3 %copy-start.18 = (bf16[256,256]{1,0:T(8,128)(2,1)}, bf16[256,256]{1,0:T(8,128)(2,1)S(1)}, u32[]{:S(2)}) copy-start(bf16[256,256]{1,0:T(8,128)(2,1)S(1)} %collective-permute-done.6.refs_7_) | copy-start | bytes 393220
  75.1 13.8 %all-to-all-start.2 = ((bf16[16,64,256]{2,1,0:T(8,128)(2,1)}), bf16[16,64,256]{2,1,0:T(8,128)(2,1)S(1)}, u32[]{:S(2)}, u32[]{:S(2)}) async-start(bf16[16,64,256]{2,1,0:T(8,128)(2,1)} %bitcast.4), calls=%async_computation.2 | async-start | bytes 1048576 | tf_op jit(solution)/shard_map/all_to_all | solution.py:198
  (23 other events, 295.0 us)
